TPU v7x, 512 devices: a whole 4x8x8 slice. The times are simulated.
512 devices in a mesh: wide: 64 (over z_lo, y, core), narrow: 8 (over x, z_hi).
Axes of the slice: x: 4, y: 8, z: 8 (z_hi: 2, z_lo: 4; z = z_hi * 4 + z_lo), core: 2. Of those that a mesh axis runs over, the one named last changes fastest.
Arguments:
- features: bfloat16 [16, 1024, 2, 1024], P(None, 'wide', None, 'narrow'), may hold values from -6 to 6
- cotangent: bfloat16 [16, 1024, 2, 1024], P(None, 'wide', None, 'narrow'), may hold values from -6 to 6
- coarse_weight: bfloat16 [32, 16, 3, 3, 3], replicated, may hold values from -0.3125 to 0.3125
- fine_weight: bfloat16 [16, 48, 3, 3, 3], replicated, may hold values from -0.15625 to 0.15625
Outputs:
- output: bfloat16 [16, 1024, 2, 1024], P(None, 'wide', None, 'narrow')
- grad_features: bfloat16 [16, 1024, 2, 1024], P(None, 'wide', None, 'narrow')
- grad_fine: float32 [16, 48, 3, 3, 3], replicated
- grad_coarse: float32 [32, 16, 3, 3, 3], replicated
All inputs are finite; a program needn't handle non-finite values.
Results may differ from a plain program's by a relative error of at most 0.012.
Values may be sent and summed in bfloat16 or wider, within the bound.
A program may use at most 64 MiB of HBM per device.

v0:
```python
import math
import jax
import jax.numpy as jnp
from jax import lax
from jax.sharding import PartitionSpec as P


def extended_2(array, sides, width):
    for axis, dim in sides:
        count, length = (lax.axis_size(axis), array.shape[dim])
        up = [(i, (i + 1) % count) for i in range(count - 1)]
        down = [(j, i) for i, j in up]
        last = lax.slice_in_dim(array, length - width, length, axis=dim)
        first = lax.slice_in_dim(array, 0, width, axis=dim)
        before = lax.ppermute(last, axis, up)
        after = lax.ppermute(first, axis, down)
        array = jnp.concatenate([before, array, after], axis=dim)
    return array


def shortened(array):
    return jax.tree.map(lambda a: a.astype(jnp.bfloat16) if a.dtype == jnp.float32 else a, array)


def correlate(padded, kernel):
    result = lax.conv_general_dilated(
        padded[None],
        kernel,
        (1, 1, 1),
        "VALID",
        dimension_numbers=("NCHWD", "OIHWD", "NCHWD"),
        preferred_element_type=jnp.float32,
    )
    return result[0]


def weight_grad(padded, grad):
    result = lax.conv_general_dilated(
        padded[:, None],
        grad[:, None],
        (1, 1, 1),
        "VALID",
        dimension_numbers=("NCHWD", "OIHWD", "NCHWD"),
        preferred_element_type=jnp.float32,
    )
    return jnp.transpose(result, (1, 0, 2, 3, 4))


def flipped(kernel):
    return jnp.transpose(kernel[:, :, ::-1, ::-1, ::-1], (1, 0, 2, 3, 4))


def pool_sum(field):
    chans, rows, planes, cols = field.shape
    return field.reshape(chans, rows // 2, 2, planes // 2, 2, cols // 2, 2).sum(axis=(2, 4, 6))


def upsample(field):
    chans, rows, planes, cols = field.shape
    spread = jnp.broadcast_to(
        field[:, :, None, :, None, :, None], (chans, rows, 2, planes, 2, cols, 2)
    )
    return spread.reshape(chans, 2 * rows, 2 * planes, 2 * cols)


def silu_slope(value):
    sig = jax.nn.sigmoid(value)
    return sig * (1.0 + value * (1.0 - sig))


def fine_padded(field):
    extended = extended_2(field, (("wide", 1), ("narrow", 3)), 1)
    return jnp.pad(extended, ((0, 0), (0, 0), (1, 1), (0, 0)))


def coarse_padded(field):
    extended = extended_2(field, ((("wide", "narrow"), 1),), 1)
    return jnp.pad(extended, ((0, 0), (0, 0), (1, 1), (1, 1)))


def into_coarse(field):
    return jax.tree.map(
        lambda part, own: part.astype(own.dtype),
        lax.all_to_all(shortened(field), "narrow", split_axis=1, concat_axis=3, tiled=True),
        field,
    )


def into_fine(field):
    return jax.tree.map(
        lambda part, own: part.astype(own.dtype),
        lax.all_to_all(shortened(field), "narrow", split_axis=3, concat_axis=1, tiled=True),
        field,
    )


def shards(features, cotangent, coarse_weight, fine_weight):
    channels = features.shape[0]
    pooled = (pool_sum(features.astype(jnp.float32)) / 8.0).astype(jnp.bfloat16)
    coarse_ext = coarse_padded(into_coarse(pooled))
    coarse_pre = correlate(coarse_ext, coarse_weight)
    coarse_act = jax.nn.silu(coarse_pre).astype(jnp.bfloat16)
    upsampled = upsample(into_fine(coarse_act))
    joined_ext = fine_padded(jnp.concatenate([features, upsampled], 0))
    cotangent_ext = fine_padded(cotangent)
    output = correlate(joined_ext, fine_weight).astype(jnp.bfloat16)
    local_fine = weight_grad(joined_ext, cotangent)
    grad_joined = correlate(cotangent_ext, flipped(fine_weight))
    grad_act = into_coarse(pool_sum(grad_joined[channels:]).astype(jnp.bfloat16))
    grad_pre = (grad_act.astype(jnp.float32) * silu_slope(coarse_pre)).astype(jnp.bfloat16)
    local_coarse = weight_grad(coarse_ext, grad_pre)
    grad_pooled = correlate(coarse_padded(grad_pre), flipped(coarse_weight)).astype(jnp.bfloat16)
    grad_features = (
        grad_joined[:channels] + upsample(into_fine(grad_pooled)).astype(jnp.float32) / 8.0
    ).astype(jnp.bfloat16)
    fine_total, coarse_total = lax.psum((local_fine, local_coarse), ("wide", "narrow"))
    all_cells = (
        features.shape[1]
        * features.shape[2]
        * features.shape[3]
        * lax.axis_size("wide")
        * lax.axis_size("narrow")
    )
    return (
        output,
        grad_features,
        fine_total / math.sqrt(all_cells),
        coarse_total / math.sqrt(all_cells // 8),
    )


def solution(mesh):
    placed = (P(None, "wide", None, "narrow"), P(None, "wide", None, "narrow"), P(), P())
    return jax.shard_map(
        shards,
        mesh=mesh,
        in_specs=placed,
        out_specs=(P(None, "wide", None, "narrow"), P(None, "wide", None, "narrow"), P(), P()),
        check_vma=False,
    )
```

profile of v0, /device:TPU:1, one launch (start us, length us, event | category | flops | bytes accessed | tf_op | source)
XLA Modules:
  0.0 639.0 jit_solution(16950988302908629010)
XLA Ops:
  7.2 0.8 fusion.97
  8.0 4.6 collective-permute-start.6
  12.6 5.5 collective-permute-start.7
  18.1 1.3 convert_reduce_fusion
  19.7 0.9 reduce_sum.25
  21.0 1.3 collective-permute-start.9
  22.3 8.1 %collective-permute-start.8 = (bf16[16,18,2,1]{3,2,1,0:T(2,128)(2,1)S(1)}, bf16[16,18,2,1]{3,2,1,0:T(2,128)(2,1)S(1)}, u32[]{:S(2)}, u32[]{:S(2)}) collective-permute-start(bf16[16,18,2,1]{3,2,1,0:T(2,128)(2,1)S(1)} %get-tuple-element.36), channel_id=1, source_target_pairs={{0,1},{1,2},{2,3},{3,4},{4,5},{5,6},{6,7},{8,9},{9,10},{10,11},{11... | collective-permute-start | bytes 3464 | tf_op jit(solution)/shard_map/ppermute | solution.py:15
  30.6 0.7 reshape.289
  31.3 10.0 %all-to-all-start = ((bf16[8,2,512]{2,1,0:T(2,128)(2,1)}), bf16[8,2,512]{2,1,0:T(2,128)(2,1)S(1)}, u32[]{:S(2)}, u32[]{:S(2)}) async-start(bf16[8,2,512]{2,1,0:T(2,128)(2,1)} %reshape.289), calls=%async_computation | async-start | bytes 32768 | tf_op jit(solution)/shard_map/all_to_all | solution.py:84
  41.3 3.8 copy.231
  45.1 1.3 fusion.54
  46.7 1.8 reshape.286
  48.5 5.1 copy.219
  53.6 1.0 slice.64
  54.7 5.0 fusion.26
  60.4 2.0 copy.221
  62.6 8.5 %collective-permute-start.1 = (bf16[16,1,1,512]{3,0,2,1:T(8,128)(2,1)S(1)}, bf16[16,1,1,512]{3,0,2,1:T(8,128)(2,1)S(1)}, u32[]{:S(2)}, u32[]{:S(2)}) collective-permute-start(bf16[16,1,1,512]{3,0,2,1:T(8,128)(2,1)S(1)} %all_to_all.11), channel_id=1, source_target_pairs={{1,0},{2,1},{3,2},{4,3},{5,4},{6,5},{7,6},{8,7},{9,8},{10,9},{11,1... | collective-permute-start | bytes 49160 | tf_op jit(solution)/shard_map/ppermute | solution.py:16
  71.1 2.1 collective-permute-start
  73.2 1.9 slice_reduce_fusion
  75.1 1.8 reduce_sum.37
  76.9 1.0 copy.222
  77.9 0.7 reshape.287
  78.6 10.8 %all-to-all-start.2 = ((bf16[8,2,1024]{2,1,0:T(2,128)(2,1)}), bf16[8,2,1024]{2,1,0:T(2,128)(2,1)S(1)}, u32[]{:S(2)}, u32[]{:S(2)}) async-start(bf16[8,2,1024]{2,1,0:T(2,128)(2,1)} %reshape.287), calls=%async_computation.2 | async-start | bytes 65536 | tf_op jit(solution)/shard_map/all_to_all | solution.py:84
  89.4 2.8 copy.220
  92.2 2.8 reshape.252
  95.0 0.8 fusion.98
  96.1 0.8 copy.204
  97.0 1.2 fusion.46
  98.2 0.8 fusion.99
  99.3 2.0 copy.233
  101.6 8.2 %collective-permute-start.11 = (bf16[32,1,1,512]{3,0,2,1:T(8,128)(2,1)S(1)}, bf16[32,1,1,512]{3,0,2,1:T(8,128)(2,1)S(1)}, u32[]{:S(2)}, u32[]{:S(2)}) collective-permute-start(bf16[32,1,1,512]{3,0,2,1:T(8,128)(2,1)S(1)} %get-tuple-element.40), channel_id=1, source_target_pairs={{1,0},{2,1},{3,2},{4,3},{5,4},{6,5},{7,6},{8,7},{9,8},{10,9},{11,1... | collective-permute-start | bytes 98312 | tf_op jit(solution)/shard_map/ppermute | solution.py:16
  109.7 1.9 collective-permute-start.10
  112.4 1.5 reduce.8
  113.9 0.8 reshape.291
  114.7 11.2 %all-to-all-start.1 = ((bf16[8,2,1024]{2,1,0:T(2,128)(2,1)}), bf16[8,2,1024]{2,1,0:T(2,128)(2,1)S(1)}, u32[]{:S(2)}, u32[]{:S(2)}) async-start(bf16[8,2,1024]{2,1,0:T(2,128)(2,1)} %reshape.291), calls=%async_computation.1 | async-start | bytes 65536 | tf_op jit(solution)/shard_map/all_to_all | solution.py:92
  126.1 5.7 fusion.101
  131.8 105.8 %psum.15 = f32[32,16,3,3,3]{0,1,4,3,2:T(8,128)S(1)} all-reduce(f32[32,16,3,3,3]{0,1,4,3,2:T(8,128)S(1)} %fusion.101), channel_id=1, replica_groups=mesh['wide'=64,'narrow'=8] {'wide','narrow'}, use_global_device_ids=true, to_apply=%region_5.6 | all-reduce | flops 13824 | bytes 110592 | tf_op jit(solution)/shard_map/psum | solution.py:116
  237.6 0.7 broadcast_multiply_fusion
  239.0 1.7 copy.225
  240.8 1.1 fusion.33
  242.3 1.5 reduce.9
  243.8 0.8 reshape.293
  244.6 3.3 all-to-all-start.3
  248.9 2.9 collective-permute-start.3
  251.8 2.6 collective-permute-start.2
  254.4 2.4 all-to-all-done.3
  258.3 1.3 collective-permute-start.5
  259.6 8.3 %collective-permute-start.4 = (bf16[48,18,2,1]{3,0,2,1:T(8,128)(2,1)S(1)}, bf16[48,18,2,1]{3,0,2,1:T(8,128)(2,1)S(1)}, u32[]{:S(2)}, u32[]{:S(2)}) collective-permute-start(bf16[48,18,2,1]{3,0,2,1:T(8,128)(2,1)S(1)} %get-tuple-element.32), channel_id=1, source_target_pairs={{0,1},{1,2},{2,3},{3,4},{4,5},{5,6},{6,7},{8,9},{9,10},{10,11},{11... | collective-permute-start | bytes 10376 | tf_op jit(solution)/shard_map/ppermute | solution.py:15
  268.0 0.8 copy.236
  268.7 5.5 collective-permute-done.5
  274.2 0.9 collective-permute-done.4
  275.2 0.8 copy-done.1
  275.9 2.0 fusion.111
  277.9 4.9 copy.240
  282.8 1.3 pad.22.clone
  284.5 6.5 %fusion.9 = bf16[16,2,8,17,16]{4,2,3,1,0:T(8,128)(2,1)} fusion(bf16[16,48,3,3,3]{1,0,4,3,2:T(8,128)(2,1)S(1)} %copy-done, bf16[48,18,4,1,7,2]{0,4,5,2,1,3:T(8,128)(2,1)S(1)} %slice.60, bf16[48,18,4,1,8,17]{0,4,5,2,1,3:T(8,128)(2,1)S(1)} %copy.213), kind=kOutput, calls=%fused_computation.12 | convolution fusion | flops 183638016 | bytes 1217536 | tf_op jit(solution)/shard_map/conv_general_dilated | solution.py:26
  291.0 2.7 copy.214
  294.4 0.7 reshape.245
  295.1 1.1 fusion.110
  296.2 8.8 %copy.230 = bf16[48,1,18,4,130]{0,1,4,3,2:T(2,128)(2,1)} copy(bf16[48,1,18,4,130]{4,0,3,2,1:T(8,128)(2,1)S(1)} %fusion.110) | data formatting | bytes 1797120 | tf_op jit(solution)/shard_map/broadcast_in_dim | solution.py:39
  305.0 31.3 %fusion.100 = f32[16,48,3,3,3]{1,0,4,3,2:T(8,128)} fusion(bf16[48,1,18,4,130]{0,1,4,3,2:T(2,128)(2,1)} %copy.230, bf16[16,1,16,2,128]{0,1,4,3,2:T(2,128)(2,1)} %copy.231), kind=kOutput, calls=%fused_computation.139 | convolution fusion | flops 169869312 | bytes 1112576 | tf_op jit(solution)/shard_map/transpose | solution.py:46
  336.3 0.8 copy.235
  337.1 293.2 %all-reduce.6.cloned.1.call-done = f32[16,48,3,3,3]{1,0,4,3,2:T(8,128)} async-done(((f32[16,48,3,3,3]{1,0,4,3,2:T(8,128)}), f32[16,48,3,3,3]{1,0,4,3,2:T(8,128)}) %all-reduce.6.cloned.1.call-update) | async-done | bytes 82960 | tf_op jit(solution)/shard_map/psum | solution.py:116
  630.3 1.6 broadcast_multiply_fusion.1
  (91 shorter events, 8.5 us)
Async XLA Ops:
  7.2 47.5 %copy-start = (bf16[16,48,3,3,3]{1,0,4,3,2:T(8,128)(2,1)S(1)}, bf16[16,48,3,3,3]{1,0,4,3,2:T(8,128)(2,1)}, u32[]{:S(2)}) copy-start(bf16[16,48,3,3,3]{1,0,4,3,2:T(8,128)(2,1)} %param.7) | copy-start | bytes 124420
  7.2 13.4 %copy-start.4 = (bf16[16,16,2,128]{3,2,1,0:T(2,128)(2,1)S(1)}, bf16[16,16,2,128]{3,2,1,0:T(2,128)(2,1)}, u32[]{:S(2)}) copy-start(bf16[16,16,2,128]{3,2,1,0:T(2,128)(2,1)} %param.5) | copy-start | bytes 393220
  7.2 34.1 %copy-start.5 = (bf16[16,16,2,128]{3,2,1,0:T(2,128)(2,1)S(1)}, bf16[16,16,2,128]{3,2,1,0:T(2,128)(2,1)}, u32[]{:S(2)}) copy-start(bf16[16,16,2,128]{3,2,1,0:T(2,128)(2,1)} %param.4) | copy-start | bytes 393220
  8.0 12.6 %collective-permute-start.6 = (bf16[16,1,2,128]{3,2,1,0:T(2,128)(2,1)S(1)}, bf16[16,1,2,128]{3,2,1,0:T(2,128)(2,1)S(1)}, u32[]{:S(2)}, u32[]{:S(2)}) collective-permute-start(bf16[16,1,2,128]{3,2,1,0:T(2,128)(2,1)S(1)} %get-tuple-element.39), channel_id=1, source_target_pairs={{0,8},{8,16},{16,24},{24,32},{32,40},{40,48},{48,56},{56,64},{64,7... | collective-permute-start | bytes 24584 | tf_op jit(solution)/shard_map/ppermute | solution.py:15
  12.6 8.1 %collective-permute-start.7 = (bf16[16,1,2,128]{3,2,1,0:T(2,128)(2,1)S(1)}, bf16[16,1,2,128]{3,2,1,0:T(2,128)(2,1)S(1)}, u32[]{:S(2)}, u32[]{:S(2)}) collective-permute-start(bf16[16,1,2,128]{3,2,1,0:T(2,128)(2,1)S(1)} %get-tuple-element.38), channel_id=1, source_target_pairs={{8,0},{16,8},{24,16},{32,24},{40,32},{48,40},{56,48},{64,56},{72,6... | collective-permute-start | bytes 24584 | tf_op jit(solution)/shard_map/ppermute | solution.py:16
  21.0 24.1 %collective-permute-start.9 = (bf16[16,18,2,1]{3,2,1,0:T(2,128)(2,1)S(1)}, bf16[16,18,2,1]{3,2,1,0:T(2,128)(2,1)S(1)}, u32[]{:S(2)}, u32[]{:S(2)}) collective-permute-start(bf16[16,18,2,1]{3,2,1,0:T(2,128)(2,1)S(1)} %get-tuple-element.37), channel_id=1, source_target_pairs={{1,0},{2,1},{3,2},{4,3},{5,4},{6,5},{7,6},{9,8},{10,9},{11,10},{12... | collective-permute-start | bytes 3464 | tf_op jit(solution)/shard_map/ppermute | solution.py:16
  22.3 22.8 %collective-permute-start.8 = (bf16[16,18,2,1]{3,2,1,0:T(2,128)(2,1)S(1)}, bf16[16,18,2,1]{3,2,1,0:T(2,128)(2,1)S(1)}, u32[]{:S(2)}, u32[]{:S(2)}) collective-permute-start(bf16[16,18,2,1]{3,2,1,0:T(2,128)(2,1)S(1)} %get-tuple-element.36), channel_id=1, source_target_pairs={{0,1},{1,2},{2,3},{3,4},{4,5},{5,6},{6,7},{8,9},{9,10},{10,11},{11... | collective-permute-start | bytes 3464 | tf_op jit(solution)/shard_map/ppermute | solution.py:15
  31.3 31.1 %all-to-all-start = ((bf16[8,2,512]{2,1,0:T(2,128)(2,1)}), bf16[8,2,512]{2,1,0:T(2,128)(2,1)S(1)}, u32[]{:S(2)}, u32[]{:S(2)}) async-start(bf16[8,2,512]{2,1,0:T(2,128)(2,1)} %reshape.289), calls=%async_computation | async-start | bytes 32768 | tf_op jit(solution)/shard_map/all_to_all | solution.py:84
  48.5 6.2 copy-start.10
  62.6 32.4 %collective-permute-start.1 = (bf16[16,1,1,512]{3,0,2,1:T(8,128)(2,1)S(1)}, bf16[16,1,1,512]{3,0,2,1:T(8,128)(2,1)S(1)}, u32[]{:S(2)}, u32[]{:S(2)}) collective-permute-start(bf16[16,1,1,512]{3,0,2,1:T(8,128)(2,1)S(1)} %all_to_all.11), channel_id=1, source_target_pairs={{1,0},{2,1},{3,2},{4,3},{5,4},{6,5},{7,6},{8,7},{9,8},{10,9},{11,1... | collective-permute-start | bytes 49160 | tf_op jit(solution)/shard_map/ppermute | solution.py:16
  71.1 23.9 %collective-permute-start = (bf16[16,1,1,512]{3,0,2,1:T(8,128)(2,1)S(1)}, bf16[16,1,1,512]{3,0,2,1:T(8,128)(2,1)}, u32[]{:S(2)}, u32[]{:S(2)}) collective-permute-start(bf16[16,1,1,512]{3,0,2,1:T(8,128)(2,1)S(1)} %all_to_all.11), channel_id=1, source_target_pairs={{0,1},{1,2},{2,3},{3,4},{4,5},{5,6},{6,7},{7,8},{8,9},{9,10},{10,1... | collective-permute-start | bytes 49160 | tf_op jit(solution)/shard_map/ppermute | solution.py:15
  78.6 22.7 %all-to-all-start.2 = ((bf16[8,2,1024]{2,1,0:T(2,128)(2,1)}), bf16[8,2,1024]{2,1,0:T(2,128)(2,1)S(1)}, u32[]{:S(2)}, u32[]{:S(2)}) async-start(bf16[8,2,1024]{2,1,0:T(2,128)(2,1)} %reshape.287), calls=%async_computation.2 | async-start | bytes 65536 | tf_op jit(solution)/shard_map/all_to_all | solution.py:84
  92.2 4.7 copy-start.8
  92.2 4.7 copy-start.9
  101.6 136.7 %collective-permute-start.11 = (bf16[32,1,1,512]{3,0,2,1:T(8,128)(2,1)S(1)}, bf16[32,1,1,512]{3,0,2,1:T(8,128)(2,1)S(1)}, u32[]{:S(2)}, u32[]{:S(2)}) collective-permute-start(bf16[32,1,1,512]{3,0,2,1:T(8,128)(2,1)S(1)} %get-tuple-element.40), channel_id=1, source_target_pairs={{1,0},{2,1},{3,2},{4,3},{5,4},{6,5},{7,6},{8,7},{9,8},{10,9},{11,1... | collective-permute-start | bytes 98312 | tf_op jit(solution)/shard_map/ppermute | solution.py:16
  109.7 128.6 %collective-permute-start.10 = (bf16[32,1,1,512]{3,0,2,1:T(8,128)(2,1)S(1)}, bf16[32,1,1,512]{3,0,2,1:T(8,128)(2,1)S(1)}, u32[]{:S(2)}, u32[]{:S(2)}) collective-permute-start(bf16[32,1,1,512]{3,0,2,1:T(8,128)(2,1)S(1)} %get-tuple-element.40), channel_id=1, source_target_pairs={{0,1},{1,2},{2,3},{3,4},{4,5},{5,6},{6,7},{7,8},{8,9},{9,10},{10,1... | collective-permute-start | bytes 98312 | tf_op jit(solution)/shard_map/ppermute | solution.py:15
  114.7 129.9 %all-to-all-start.1 = ((bf16[8,2,1024]{2,1,0:T(2,128)(2,1)}), bf16[8,2,1024]{2,1,0:T(2,128)(2,1)S(1)}, u32[]{:S(2)}, u32[]{:S(2)}) async-start(bf16[8,2,1024]{2,1,0:T(2,128)(2,1)} %reshape.291), calls=%async_computation.1 | async-start | bytes 65536 | tf_op jit(solution)/shard_map/all_to_all | solution.py:92
  240.7 1.3 copy-start.7
  244.6 12.2 %all-to-all-start.3 = ((bf16[8,2,512]{2,1,0:T(2,128)(2,1)}), bf16[8,2,512]{2,1,0:T(2,128)(2,1)S(1)}, u32[]{:S(2)}, u32[]{:S(2)}) async-start(bf16[8,2,512]{2,1,0:T(2,128)(2,1)} %reshape.293), calls=%async_computation.3 | async-start | bytes 32768 | tf_op jit(solution)/shard_map/all_to_all | solution.py:92
  247.9 382.4 %all-reduce.6.cloned.1.call-start = ((), (), s32[]{:S(2)}) async-start(), calls=%async_computation.4 | async-start | bytes 442368 | tf_op jit(solution)/shard_map/psum | solution.py:116
  248.9 9.2 %collective-permute-start.3 = (bf16[48,1,2,128]{3,0,2,1:T(8,128)(2,1)S(1)}, bf16[48,1,2,128]{3,0,2,1:T(8,128)(2,1)S(1)}, u32[]{:S(2)}, u32[]{:S(2)}) collective-permute-start(bf16[48,1,2,128]{3,0,2,1:T(8,128)(2,1)S(1)} %get-tuple-element.35), channel_id=1, source_target_pairs={{8,0},{16,8},{24,16},{32,24},{40,32},{48,40},{56,48},{64,56},{72,6... | collective-permute-start | bytes 73736 | tf_op jit(solution)/shard_map/ppermute | solution.py:16
  251.8 6.3 collective-permute-start.2
  257.3 10.6 %copy-start.3 = (f32[16,2,1,136,16]{3,4,1,0,2:T(8,128)S(1)}, f32[16,2,1,136,16]{3,4,1,0,2:T(8,128)}, u32[]{:S(2)}) copy-start(f32[16,2,1,136,16]{3,4,1,0,2:T(8,128)} %reshape.252) | copy-start | bytes 835588
  258.3 15.9 %collective-permute-start.5 = (bf16[48,18,2,1]{3,0,2,1:T(8,128)(2,1)S(1)}, bf16[48,18,2,1]{3,0,2,1:T(8,128)(2,1)S(1)}, u32[]{:S(2)}, u32[]{:S(2)}) collective-permute-start(bf16[48,18,2,1]{3,0,2,1:T(8,128)(2,1)S(1)} %get-tuple-element.33), channel_id=1, source_target_pairs={{1,0},{2,1},{3,2},{4,3},{5,4},{6,5},{7,6},{9,8},{10,9},{11,10},{12... | collective-permute-start | bytes 10376 | tf_op jit(solution)/shard_map/ppermute | solution.py:16
  259.6 15.6 %collective-permute-start.4 = (bf16[48,18,2,1]{3,0,2,1:T(8,128)(2,1)S(1)}, bf16[48,18,2,1]{3,0,2,1:T(8,128)(2,1)S(1)}, u32[]{:S(2)}, u32[]{:S(2)}) collective-permute-start(bf16[48,18,2,1]{3,0,2,1:T(8,128)(2,1)S(1)} %get-tuple-element.32), channel_id=1, source_target_pairs={{0,1},{1,2},{2,3},{3,4},{4,5},{5,6},{6,7},{8,9},{9,10},{10,11},{11... | collective-permute-start | bytes 10376 | tf_op jit(solution)/shard_map/ppermute | solution.py:15
  275.2 0.8 copy-start.1
  284.5 9.3 %copy-start.6 = (pred[8,17]{1,0:T(8,128)(4,1)S(1)}, pred[8,17]{1,0:T(8,128)(4,1)}, u32[]{:S(2)}) copy-start(pred[8,17]{1,0:T(8,128)(4,1)} %constant.46) | copy-start | bytes 412
  293.8 1.3 copy-start.2
Sparse Core Ops, SparseCore 0:
  336.4 293.8 all-reduce.5
where the time goes:
time: 648 us; the launch traced here: 639 us
  waiting for transfers between devices  302 us (47%)
  blocking collectives  106 us (16%)
  starting transfers between devices  90.7 us (14%)
  local copies, waits for them, and re-layouts  56.7 us (9%)
  matrix products  50.9 us (8%)
  other arithmetic  18 us (3%)
  between operations  14.9 us (2%)
    psum x1, waiting for transfers between devices, shards(): lax.psum((local_fine, local_coarse), ('wide', 'narrow'))  293 us
    psum x1, blocking collectives, shards(): lax.psum((local_fine, local_coarse), ('wide', 'narrow'))  106 us
    transpose x2, matrix products, weight_grad(): return jnp.transpose(result, (1, 0, 2, 3, 4))  37 us
    ppermute x6, starting transfers between devices, extended_2(): before = lax.ppermute(last, axis, up)  27.7 us
    ppermute x6, starting transfers between devices, extended_2(): after = lax.ppermute(first, axis, down)  27.6 us
    conv_general_dilated x19, local copies, waits for them, and re-layouts, correlate(): lax.conv_general_dilated(padded[None], kernel, (1, 1, 1), 'VALID', dimens...  23.1 us
    all_to_all x2, starting transfers between devices, into_coarse(): lax.all_to_all(shortened(field), 'narrow', split_axis=1, concat_axis=3, t...  20.8 us
    all_to_all x2, starting transfers between devices, into_fine(): lax.all_to_all(shortened(field), 'narrow', split_axis=3, concat_axis=1, t...  14.5 us
  transfers between devices with their start and end apart: 17, of which 4 were waited for; matrix products, arithmetic and copies ran while one was open for 10% of the time, Pallas kernels for 0%

commit v1 on v0

--- a/solution.py
+++ b/solution.py
@@ -3,6 +3,11 @@
 import jax.numpy as jnp
 from jax import lax
 from jax.sharding import PartitionSpec as P
+
+
+def axis_by_axis(value_2, axis_one, axis_two):
+    half = lax.psum(value_2, axis_one)
+    return lax.psum(half, axis_two)
 
 
 def extended_2(array, sides, width):
@@ -113,7 +118,7 @@
     grad_features = (
         grad_joined[:channels] + upsample(into_fine(grad_pooled)).astype(jnp.float32) / 8.0
     ).astype(jnp.bfloat16)
-    fine_total, coarse_total = lax.psum((local_fine, local_coarse), ("wide", "narrow"))
+    fine_total, coarse_total = axis_by_axis((local_fine, local_coarse), "wide", "narrow")
     all_cells = (
         features.shape[1]
         * features.shape[2]

time: 648 us -> 1200 us (1.85)
  waiting for transfers between devices: 302 us -> 604 us
  blocking collectives: 106 us -> 340 us
    psum x1 -> x2, waiting for transfers between devices: 293 us -> 599 us  [the longest x1 492 us: axis_by_axis(): half = lax.psum(value_2, axis_one)]
    psum x1 -> x2, blocking collectives: 106 us -> 340 us  [the longest x1 261 us: axis_by_axis(): half = lax.psum(value_2, axis_one)]
    ppermute x6, starting transfers between devices: 27.6 us -> 39.9 us  [extended_2(): after = lax.ppermute(first, axis, down)]
  transfers between devices with their start and end apart: 17 -> 18, of which waited for: 4 -> 4; matrix products, arithmetic and copies ran while one was open for 10% -> 6% of each run, Pallas kernels for 0% -> 0%
where the time goes in v1:
time: 1200 us; the launch traced here: 1190 us
  waiting for transfers between devices  604 us (50%)
  blocking collectives  340 us (28%)
  starting transfers between devices  102 us (8%)
  local copies, waits for them, and re-layouts  58.4 us (5%)
  matrix products  51.6 us (4%)
  other arithmetic  21.1 us (2%)
  between operations  15.1 us (1%)
    psum x1, waiting for transfers between devices, axis_by_axis(): half = lax.psum(value_2, axis_one)  492 us
    psum x1, blocking collectives, axis_by_axis(): half = lax.psum(value_2, axis_one)  261 us
    psum x1, waiting for transfers between devices, axis_by_axis(): return lax.psum(half, axis_two)  107 us
    psum x1, blocking collectives, axis_by_axis(): return lax.psum(half, axis_two)  79.1 us
    ppermute x6, starting transfers between devices, extended_2(): after = lax.ppermute(first, axis, down)  39.9 us
    transpose x2, matrix products, weight_grad(): return jnp.transpose(result, (1, 0, 2, 3, 4))  37.7 us
    ppermute x6, starting transfers between devices, extended_2(): before = lax.ppermute(last, axis, up)  26.8 us
  transfers between devices with their start and end apart: 18, of which 4 were waited for; matrix products, arithmetic and copies ran while one was open for 6% of the time, Pallas kernels for 0%

profile of v1, /device:TPU:1, one launch (start us, length us, event | category | flops | bytes accessed | tf_op | source)
XLA Modules:
  0.0 1191.7 jit_solution(4838750973193352397)
XLA Ops:
  7.2 0.8 fusion.97
  8.0 4.6 collective-permute-start.6
  12.6 5.5 collective-permute-start.7
  18.1 1.3 convert_reduce_fusion
  19.7 0.9 reduce_sum.25
  21.0 1.3 collective-permute-start.9
  22.3 8.1 collective-permute-start.8
  31.3 10.0 all-to-all-start
  41.3 3.8 copy.231
  45.1 1.3 fusion.54
  46.7 1.8 reshape.286
  48.6 5.0 copy.219
  53.6 1.0 slice.64
  54.7 5.0 fusion.26
  60.3 2.0 copy.221
  62.6 8.5 collective-permute-start.1
  71.1 2.2 collective-permute-start
  73.3 1.9 slice_reduce_fusion
  75.2 1.8 reduce_sum.37
  76.9 1.0 copy.222
  78.7 10.8 all-to-all-start.2
  89.5 2.8 copy.220
  92.3 2.1 reshape.252
  94.5 0.8 fusion.98
  95.6 0.8 copy.204
  96.4 1.2 fusion.46
  97.6 0.8 fusion.99
  98.7 2.0 copy.233
  101.0 8.2 collective-permute-start.11
  109.2 1.9 collective-permute-start.10
  112.5 2.1 reduce.8
  114.6 1.7 reshape.291
  116.3 11.2 all-to-all-start.1
  127.4 0.9 fusion.74
  128.5 6.4 fusion.101
  134.9 260.6 %psum.30 = f32[32,16,3,3,3]{0,1,4,3,2:T(8,128)S(1)} all-reduce(f32[32,16,3,3,3]{0,1,4,3,2:T(8,128)} %fusion.101), channel_id=1, replica_groups=mesh['wide'=64,'narrow'=8] {'wide'}, use_global_device_ids=true, to_apply=%region_6.7 | all-reduce | flops 13824 | bytes 110592 | tf_op jit(solution)/shard_map/psum | solution.py:9
  395.5 79.1 %psum.31 = f32[32,16,3,3,3]{0,1,4,3,2:T(8,128)S(1)} all-reduce(f32[32,16,3,3,3]{0,1,4,3,2:T(8,128)S(1)} %psum.30), channel_id=1, replica_groups=mesh['wide'=64,'narrow'=8] {'narrow'}, use_global_device_ids=true, to_apply=%region_7.8 | all-reduce | flops 13824 | bytes 110592 | tf_op jit(solution)/shard_map/psum | solution.py:10
  475.4 0.9 fusion.55
  476.9 1.7 copy.225
  478.6 1.1 fusion.33
  480.2 1.4 reduce.9
  481.6 0.8 reshape.293
  482.3 3.3 all-to-all-start.3
  485.7 0.9 reshape.292
  487.4 15.2 %collective-permute-start.3 = (bf16[48,1,2,128]{3,0,2,1:T(8,128)(2,1)S(1)}, bf16[48,1,2,128]{3,0,2,1:T(8,128)(2,1)S(1)}, u32[]{:S(2)}, u32[]{:S(2)}) collective-permute-start(bf16[48,1,2,128]{3,0,2,1:T(8,128)(2,1)S(1)} %get-tuple-element.35), channel_id=1, source_target_pairs={{8,0},{16,8},{24,16},{32,24},{40,32},{48,40},{56,48},{64,56},{72,6... | collective-permute-start | bytes 73736 | tf_op jit(solution)/shard_map/ppermute | solution.py:21
  502.6 1.9 collective-permute-start.2
  506.0 1.3 collective-permute-start.5
  507.3 8.1 collective-permute-start.4
  515.4 0.8 copy.236
  516.2 2.9 collective-permute-done.5
  519.1 1.5 collective-permute-done.4
  520.6 0.8 copy-done.2
  521.3 2.0 fusion.111
  523.3 4.9 copy.240
  528.2 1.3 pad.22.clone
  529.9 6.5 fusion.9
  536.4 2.7 copy.214
  539.2 2.1 fusion.110
  541.3 8.8 copy.230
  550.2 31.3 %fusion.100 = f32[16,48,3,3,3]{1,0,4,3,2:T(8,128)} fusion(bf16[48,1,18,4,130]{0,1,4,3,2:T(2,128)(2,1)} %copy.230, bf16[16,1,16,2,128]{0,1,4,3,2:T(2,128)(2,1)} %copy.231), kind=kOutput, calls=%fused_computation.139 | convolution fusion | flops 169869312 | bytes 1112576 | tf_op jit(solution)/shard_map/transpose | solution.py:51
  582.9 492.1 %all-reduce.7.cloned.1.call-done = f32[16,48,3,3,3]{1,0,4,3,2:T(8,128)} async-done(((f32[16,48,3,3,3]{1,0,4,3,2:T(8,128)}), f32[16,48,3,3,3]{1,0,4,3,2:T(8,128)}) %all-reduce.7.cloned.1.call-update) | async-done | bytes 82960 | tf_op jit(solution)/shard_map/psum | solution.py:9
  1075.0 0.8 copy.235
  1075.8 107.1 %all-reduce.9.cloned.1.call-done = f32[16,48,3,3,3]{1,0,4,3,2:T(8,128)} async-done(((f32[16,48,3,3,3]{1,0,4,3,2:T(8,128)}), f32[16,48,3,3,3]{1,0,4,3,2:T(8,128)}) %all-reduce.9.cloned.1.call-update) | async-done | bytes 82960 | tf_op jit(solution)/shard_map/psum | solution.py:10
  1182.9 1.6 broadcast_multiply_fusion.1
  (95 shorter events, 11.7 us)
Async XLA Ops:
  7.2 47.5 %copy-start = (bf16[16,48,3,3,3]{1,0,4,3,2:T(8,128)(2,1)S(1)}, bf16[16,48,3,3,3]{1,0,4,3,2:T(8,128)(2,1)}, u32[]{:S(2)}) copy-start(bf16[16,48,3,3,3]{1,0,4,3,2:T(8,128)(2,1)} %param.7) | copy-start | bytes 124420
  7.2 13.4 %copy-start.3 = (bf16[16,16,2,128]{3,2,1,0:T(2,128)(2,1)S(1)}, bf16[16,16,2,128]{3,2,1,0:T(2,128)(2,1)}, u32[]{:S(2)}) copy-start(bf16[16,16,2,128]{3,2,1,0:T(2,128)(2,1)} %param.5) | copy-start | bytes 393220
  7.2 34.1 %copy-start.4 = (bf16[16,16,2,128]{3,2,1,0:T(2,128)(2,1)S(1)}, bf16[16,16,2,128]{3,2,1,0:T(2,128)(2,1)}, u32[]{:S(2)}) copy-start(bf16[16,16,2,128]{3,2,1,0:T(2,128)(2,1)} %param.4) | copy-start | bytes 393220
  8.0 12.6 %collective-permute-start.6 = (bf16[16,1,2,128]{3,2,1,0:T(2,128)(2,1)S(1)}, bf16[16,1,2,128]{3,2,1,0:T(2,128)(2,1)S(1)}, u32[]{:S(2)}, u32[]{:S(2)}) collective-permute-start(bf16[16,1,2,128]{3,2,1,0:T(2,128)(2,1)S(1)} %get-tuple-element.39), channel_id=1, source_target_pairs={{0,8},{8,16},{16,24},{24,32},{32,40},{40,48},{48,56},{56,64},{64,7... | collective-permute-start | bytes 24584 | tf_op jit(solution)/shard_map/ppermute | solution.py:20
  12.6 8.1 collective-permute-start.7
  21.0 24.1 %collective-permute-start.9 = (bf16[16,18,2,1]{3,2,1,0:T(2,128)(2,1)S(1)}, bf16[16,18,2,1]{3,2,1,0:T(2,128)(2,1)S(1)}, u32[]{:S(2)}, u32[]{:S(2)}) collective-permute-start(bf16[16,18,2,1]{3,2,1,0:T(2,128)(2,1)S(1)} %get-tuple-element.37), channel_id=1, source_target_pairs={{1,0},{2,1},{3,2},{4,3},{5,4},{6,5},{7,6},{9,8},{10,9},{11,10},{12... | collective-permute-start | bytes 3464 | tf_op jit(solution)/shard_map/ppermute | solution.py:21
  22.3 22.8 %collective-permute-start.8 = (bf16[16,18,2,1]{3,2,1,0:T(2,128)(2,1)S(1)}, bf16[16,18,2,1]{3,2,1,0:T(2,128)(2,1)S(1)}, u32[]{:S(2)}, u32[]{:S(2)}) collective-permute-start(bf16[16,18,2,1]{3,2,1,0:T(2,128)(2,1)S(1)} %get-tuple-element.36), channel_id=1, source_target_pairs={{0,1},{1,2},{2,3},{3,4},{4,5},{5,6},{6,7},{8,9},{9,10},{10,11},{11... | collective-permute-start | bytes 3464 | tf_op jit(solution)/shard_map/ppermute | solution.py:20
  31.3 31.1 %all-to-all-start = ((bf16[8,2,512]{2,1,0:T(2,128)(2,1)}), bf16[8,2,512]{2,1,0:T(2,128)(2,1)S(1)}, u32[]{:S(2)}, u32[]{:S(2)}) async-start(bf16[8,2,512]{2,1,0:T(2,128)(2,1)} %reshape.289), calls=%async_computation | async-start | bytes 32768 | tf_op jit(solution)/shard_map/all_to_all | solution.py:89
  48.5 6.1 copy-start.10
  62.6 31.9 %collective-permute-start.1 = (bf16[16,1,1,512]{3,0,2,1:T(8,128)(2,1)S(1)}, bf16[16,1,1,512]{3,0,2,1:T(8,128)(2,1)S(1)}, u32[]{:S(2)}, u32[]{:S(2)}) collective-permute-start(bf16[16,1,1,512]{3,0,2,1:T(8,128)(2,1)S(1)} %all_to_all.11), channel_id=1, source_target_pairs={{1,0},{2,1},{3,2},{4,3},{5,4},{6,5},{7,6},{8,7},{9,8},{10,9},{11,1... | collective-permute-start | bytes 49160 | tf_op jit(solution)/shard_map/ppermute | solution.py:21
  71.1 23.4 %collective-permute-start = (bf16[16,1,1,512]{3,0,2,1:T(8,128)(2,1)S(1)}, bf16[16,1,1,512]{3,0,2,1:T(8,128)(2,1)}, u32[]{:S(2)}, u32[]{:S(2)}) collective-permute-start(bf16[16,1,1,512]{3,0,2,1:T(8,128)(2,1)S(1)} %all_to_all.11), channel_id=1, source_target_pairs={{0,1},{1,2},{2,3},{3,4},{4,5},{5,6},{6,7},{7,8},{8,9},{9,10},{10,1... | collective-permute-start | bytes 49160 | tf_op jit(solution)/shard_map/ppermute | solution.py:20
  78.7 22.1 %all-to-all-start.2 = ((bf16[8,2,1024]{2,1,0:T(2,128)(2,1)}), bf16[8,2,1024]{2,1,0:T(2,128)(2,1)S(1)}, u32[]{:S(2)}, u32[]{:S(2)}) async-start(bf16[8,2,1024]{2,1,0:T(2,128)(2,1)} %reshape.287), calls=%async_computation.2 | async-start | bytes 65536 | tf_op jit(solution)/shard_map/all_to_all | solution.py:89
  92.3 4.1 copy-start.7
  92.3 4.1 copy-start.9
  101.0 374.3 %collective-permute-start.11 = (bf16[32,1,1,512]{3,0,2,1:T(8,128)(2,1)S(1)}, bf16[32,1,1,512]{3,0,2,1:T(8,128)(2,1)}, u32[]{:S(2)}, u32[]{:S(2)}) collective-permute-start(bf16[32,1,1,512]{3,0,2,1:T(8,128)(2,1)S(1)} %get-tuple-element.40), channel_id=1, source_target_pairs={{1,0},{2,1},{3,2},{4,3},{5,4},{6,5},{7,6},{8,7},{9,8},{10,9},{11,1... | collective-permute-start | bytes 98312 | tf_op jit(solution)/shard_map/ppermute | solution.py:21
  109.2 366.1 %collective-permute-start.10 = (bf16[32,1,1,512]{3,0,2,1:T(8,128)(2,1)S(1)}, bf16[32,1,1,512]{3,0,2,1:T(8,128)(2,1)}, u32[]{:S(2)}, u32[]{:S(2)}) collective-permute-start(bf16[32,1,1,512]{3,0,2,1:T(8,128)(2,1)S(1)} %get-tuple-element.40), channel_id=1, source_target_pairs={{0,1},{1,2},{2,3},{3,4},{4,5},{5,6},{6,7},{7,8},{8,9},{9,10},{10,1... | collective-permute-start | bytes 98312 | tf_op jit(solution)/shard_map/ppermute | solution.py:20
  116.3 366.1 %all-to-all-start.1 = ((bf16[8,2,1024]{2,1,0:T(2,128)(2,1)}), bf16[8,2,1024]{2,1,0:T(2,128)(2,1)}, u32[]{:S(2)}, u32[]{:S(2)}) async-start(bf16[8,2,1024]{2,1,0:T(2,128)(2,1)} %reshape.291), calls=%async_computation.1 | async-start | bytes 65536 | tf_op jit(solution)/shard_map/all_to_all | solution.py:97
  395.5 83.1 %copy-start.8 = (bf16[32,16,3,3,3]{0,1,4,3,2:T(8,128)(2,1)S(1)}, bf16[32,16,3,3,3]{0,1,4,3,2:T(8,128)(2,1)}, u32[]{:S(2)}) copy-start(bf16[32,16,3,3,3]{0,1,4,3,2:T(8,128)(2,1)} %param.6) | copy-start | bytes 82948
  478.6 1.3 copy-start.6
  482.3 22.2 %all-to-all-start.3 = ((bf16[8,2,512]{2,1,0:T(2,128)(2,1)}), bf16[8,2,512]{2,1,0:T(2,128)(2,1)S(1)}, u32[]{:S(2)}, u32[]{:S(2)}) async-start(bf16[8,2,512]{2,1,0:T(2,128)(2,1)} %reshape.293), calls=%async_computation.3 | async-start | bytes 32768 | tf_op jit(solution)/shard_map/all_to_all | solution.py:97
  485.7 589.2 %all-reduce.7.cloned.1.call-start = ((), (), s32[]{:S(2)}) async-start(), calls=%async_computation.4 | async-start | bytes 442368 | tf_op jit(solution)/shard_map/psum | solution.py:9
  487.4 18.4 %collective-permute-start.3 = (bf16[48,1,2,128]{3,0,2,1:T(8,128)(2,1)S(1)}, bf16[48,1,2,128]{3,0,2,1:T(8,128)(2,1)S(1)}, u32[]{:S(2)}, u32[]{:S(2)}) collective-permute-start(bf16[48,1,2,128]{3,0,2,1:T(8,128)(2,1)S(1)} %get-tuple-element.35), channel_id=1, source_target_pairs={{8,0},{16,8},{24,16},{32,24},{40,32},{48,40},{56,48},{64,56},{72,6... | collective-permute-start | bytes 73736 | tf_op jit(solution)/shard_map/ppermute | solution.py:21
  502.6 3.2 collective-permute-start.2
  506.0 13.1 %collective-permute-start.5 = (bf16[48,18,2,1]{3,0,2,1:T(8,128)(2,1)S(1)}, bf16[48,18,2,1]{3,0,2,1:T(8,128)(2,1)S(1)}, u32[]{:S(2)}, u32[]{:S(2)}) collective-permute-start(bf16[48,18,2,1]{3,0,2,1:T(8,128)(2,1)S(1)} %get-tuple-element.33), channel_id=1, source_target_pairs={{1,0},{2,1},{3,2},{4,3},{5,4},{6,5},{7,6},{9,8},{10,9},{11,10},{12... | collective-permute-start | bytes 10376 | tf_op jit(solution)/shard_map/ppermute | solution.py:21
  507.3 13.3 %collective-permute-start.4 = (bf16[48,18,2,1]{3,0,2,1:T(8,128)(2,1)S(1)}, bf16[48,18,2,1]{3,0,2,1:T(8,128)(2,1)S(1)}, u32[]{:S(2)}, u32[]{:S(2)}) collective-permute-start(bf16[48,18,2,1]{3,0,2,1:T(8,128)(2,1)S(1)} %get-tuple-element.32), channel_id=1, source_target_pairs={{0,1},{1,2},{2,3},{3,4},{4,5},{5,6},{6,7},{8,9},{9,10},{10,11},{11... | collective-permute-start | bytes 10376 | tf_op jit(solution)/shard_map/ppermute | solution.py:20
  519.1 1.5 copy-start.1
  520.6 0.8 copy-start.2
  550.2 31.4 %copy-start.5 = (pred[8,17]{1,0:T(8,128)(4,1)S(1)}, pred[8,17]{1,0:T(8,128)(4,1)}, u32[]{:S(2)}) copy-start(pred[8,17]{1,0:T(8,128)(4,1)} %constant.46) | copy-start | bytes 412
  581.5 601.3 %all-reduce.9.cloned.1.call-start = ((), (), s32[]{:S(2)}) async-start(), calls=%async_computation.5 | async-start | bytes 442368 | tf_op jit(solution)/shard_map/psum | solution.py:10
Sparse Core Ops, SparseCore 0:
  581.6 493.2 all-reduce.6
  1078.1 104.6 all-reduce.8
